TPU v7x, 32 devices: a whole 2x2x4 slice. The times are simulated.
32 devices in a mesh: dp: 8 (over y, x, core), mem: 4 (over z).
Axes of the slice: x: 2, y: 2, z: 4, core: 2. Of those that a mesh axis runs over, the one named last changes fastest.
Arguments:
- decoder_input: bfloat16 [32, 1024, 512], P(('dp', 'mem')), may hold values from -6 to 6
- timesteps: int32 [32], P(('dp', 'mem')), may hold values from 0 to 49
- memory: bfloat16 [32, 1024, 512], P('dp', 'mem'), may hold values from -6 to 6
- cotangent: bfloat16 [32, 1024, 512], P(('dp', 'mem')), may hold values from -6 to 6
- time_weight: bfloat16 [512, 512], P('dp'), may hold values from -0.25 to 0.25
- attn_query: bfloat16 [512, 512], P('dp'), may hold values from -0.375 to 0.375
- attn_key: bfloat16 [512, 512], P('dp'), may hold values from -0.25 to 0.25
- attn_value: bfloat16 [512, 512], P('dp'), may hold values from -0.25 to 0.25
- attn_out: bfloat16 [512, 512], P('dp'), may hold values from -4 to 4
- cross_query: bfloat16 [512, 512], P('dp'), may hold values from -0.375 to 0.375
- cross_key: bfloat16 [512, 512], P('dp'), may hold values from -0.25 to 0.25
- cross_value: bfloat16 [512, 512], P('dp'), may hold values from -0.25 to 0.25
- cross_out: bfloat16 [512, 512], P('dp'), may hold values from -4 to 4
- ffn_in: bfloat16 [512, 2048], P('dp'), may hold values from -0.25 to 0.25
- ffn_out: bfloat16 [2048, 512], P('dp'), may hold values from -0.125 to 0.125
- norm_gains: float32 [512, 3], replicated, may hold values from 0.25 to 1.75
Outputs:
- layer_output: bfloat16 [32, 1024, 512], P(('dp', 'mem'))
- input_grad: bfloat16 [32, 1024, 512], P(('dp', 'mem'))
- memory_grad: bfloat16 [32, 1024, 512], P('dp', 'mem')
- grad_time: float32 [512, 512], P('dp', 'mem')
- grad_attn_query: float32 [512, 512], P('dp', 'mem')
- grad_attn_key: float32 [512, 512], P('dp', 'mem')
- grad_attn_value: float32 [512, 512], P('dp', 'mem')
- grad_attn_out: float32 [512, 512], P('dp', 'mem')
- grad_cross_query: float32 [512, 512], P('dp', 'mem')
- grad_cross_key: float32 [512, 512], P('dp', 'mem')
- grad_cross_value: float32 [512, 512], P('dp', 'mem')
- grad_cross_out: float32 [512, 512], P('dp', 'mem')
- grad_ffn_in: float32 [512, 2048], P('dp', 'mem')
- grad_ffn_out: float32 [2048, 512], P('dp', 'mem')
- grad_gains: float32 [512, 3], P('dp')
All inputs are finite; a program needn't handle non-finite values.
Results may differ from a plain program's by a relative error of at most 0.022.
Values may be sent and summed in bfloat16 or wider, within the bound.
No kernel may reach another device: no remote copies, remote signals or barrier semaphores. Data moves between devices by JAX's collectives and lax.ppermute only.
A program may use at most 320 MiB of HBM per device.

v0:
```python
import math

import jax
import jax.numpy as jnp
from jax import lax
from jax.sharding import PartitionSpec as P

D = 512
HEADS = 8
FF = 2048


def shortened(x):
    return jax.tree.map(lambda a: a.astype(jnp.bfloat16) if a.dtype == jnp.float32 else a, x)


def layer_norm(values, gain_vec):
    row_mean = jnp.mean(values, axis=-1, keepdims=True)
    centred = values - row_mean
    variance = jnp.mean(centred * centred, axis=-1, keepdims=True)
    return centred * lax.rsqrt(variance + 1e-05) * gain_vec


def step_signal(step_ids, feat_width):
    half_width = feat_width // 2
    frequency = jnp.exp(-math.log(10000.0) * jnp.arange(half_width, dtype=jnp.float32) / half_width)
    angles = step_ids.astype(jnp.float32)[:, None] * frequency[None, :]
    return jnp.concatenate([jnp.sin(angles), jnp.cos(angles)], axis=1)


def matmul(first_op, second_op):
    return jnp.dot(first_op, second_op, preferred_element_type=jnp.float32)


def matmul_tn(first_op, second_op):
    return lax.dot_general(
        first_op, second_op, (((0,), (0,)), ((), ())), preferred_element_type=jnp.float32
    )


def matmul_nt(first_op, second_op):
    return lax.dot_general(
        first_op, second_op, (((1,), (1,)), ((), ())), preferred_element_type=jnp.float32
    )


def split_heads(matrix, head_count):
    return matrix.reshape(matrix.shape[0], head_count, matrix.shape[1] // head_count)


def attend_forward(queries, keys, values, head_count):
    length_here, feat_width = queries.shape
    score_scale = 1.0 / math.sqrt(feat_width // head_count)
    block_rows = math.gcd(length_here, 512)
    key_heads = split_heads(keys, head_count)
    value_heads = split_heads(values, head_count)
    outputs = []
    totals = []
    for offset in range(0, length_here, block_rows):
        query_heads = split_heads(queries[offset : offset + block_rows], head_count)
        scores = (
            jnp.einsum("qhd,khd->hqk", query_heads, key_heads, preferred_element_type=jnp.float32)
            * score_scale
        )
        row_peak = jnp.max(scores, axis=-1, keepdims=True)
        exp_scores = jnp.exp(scores - row_peak)
        row_total = jnp.sum(exp_scores, axis=-1, keepdims=True)
        prob_low = (exp_scores / row_total).astype(jnp.bfloat16)
        mixed_heads = jnp.einsum(
            "hqk,khd->qhd", prob_low, value_heads, preferred_element_type=jnp.float32
        )
        outputs.append(mixed_heads.reshape(block_rows, feat_width))
        totals.append(row_peak + jnp.log(row_total))
    return (jnp.concatenate(outputs, 0).astype(jnp.bfloat16), jnp.concatenate(totals, 1))


def attend_backward(queries, keys, values, log_totals, grad_out, head_count):
    length_here, feat_width = queries.shape
    score_scale = 1.0 / math.sqrt(feat_width // head_count)
    block_rows = math.gcd(length_here, 512)
    key_heads = split_heads(keys, head_count)
    value_heads = split_heads(values, head_count)
    grad_keys = jnp.zeros(key_heads.shape, jnp.float32)
    grad_values = jnp.zeros(value_heads.shape, jnp.float32)
    grad_queries = []
    for offset in range(0, length_here, block_rows):
        query_heads = split_heads(queries[offset : offset + block_rows], head_count)
        grad_heads = split_heads(grad_out[offset : offset + block_rows], head_count)
        scores = (
            jnp.einsum("qhd,khd->hqk", query_heads, key_heads, preferred_element_type=jnp.float32)
            * score_scale
        )
        probs_full = jnp.exp(scores - log_totals[:, offset : offset + block_rows])
        grad_probs = jnp.einsum(
            "qhd,khd->hqk", grad_heads, value_heads, preferred_element_type=jnp.float32
        )
        row_inner = jnp.sum(probs_full * grad_probs, axis=-1, keepdims=True)
        grad_scores = (probs_full * (grad_probs - row_inner)).astype(jnp.bfloat16)
        grad_values = grad_values + jnp.einsum(
            "hqk,qhd->khd",
            probs_full.astype(jnp.bfloat16),
            grad_heads,
            preferred_element_type=jnp.float32,
        )
        grad_keys = (
            grad_keys
            + jnp.einsum(
                "hqk,qhd->khd", grad_scores, query_heads, preferred_element_type=jnp.float32
            )
            * score_scale
        )
        grad_block = (
            jnp.einsum("hqk,khd->qhd", grad_scores, key_heads, preferred_element_type=jnp.float32)
            * score_scale
        )
        grad_queries.append(grad_block.reshape(block_rows, feat_width))
    grad_q_all = jnp.concatenate(grad_queries, 0).astype(jnp.bfloat16)
    return (
        grad_q_all,
        grad_keys.reshape(keys.shape).astype(jnp.bfloat16),
        grad_values.reshape(values.shape).astype(jnp.bfloat16),
    )


def attend_segments(queries, keys, values, head_count):
    result_here, total_here = attend_forward(queries, keys[0], values[0], head_count)
    totals = [total_here]
    return (result_here, totals)


def attend_segments_back(queries, keys, values, totals, grad_out, head_count):
    grad_q_here, grad_k_here, grad_v_here = attend_backward(
        queries, keys[0], values[0], totals[0], grad_out, head_count
    )
    grad_k_list = [grad_k_here]
    grad_v_list = [grad_v_here]
    return (grad_q_here, jnp.stack(grad_k_list, 0), jnp.stack(grad_v_list, 0))


def per_device(
    decoder_input,
    timesteps,
    memory,
    cotangent,
    time_weight,
    attn_query,
    attn_key,
    attn_value,
    attn_out,
    cross_query,
    cross_key,
    cross_value,
    cross_out,
    ffn_in,
    ffn_out,
    norm_gains,
):
    seg_count, seg_len, feat_width = decoder_input.shape
    row_count = seg_count * seg_len
    bf16 = jnp.bfloat16
    gathered = (
        lax.all_gather(time_weight, "dp", axis=0, tiled=True),
        lax.all_gather(attn_query, "dp", axis=0, tiled=True),
        lax.all_gather(attn_key, "dp", axis=0, tiled=True),
        lax.all_gather(attn_value, "dp", axis=0, tiled=True),
        lax.all_gather(attn_out, "dp", axis=0, tiled=True),
        lax.all_gather(cross_query, "dp", axis=0, tiled=True),
        lax.all_gather(cross_key, "dp", axis=0, tiled=True),
        lax.all_gather(cross_value, "dp", axis=0, tiled=True),
        lax.all_gather(cross_out, "dp", axis=0, tiled=True),
        lax.all_gather(ffn_in, "dp", axis=0, tiled=True),
        lax.all_gather(ffn_out, "dp", axis=0, tiled=True),
    )
    w_time, w_query, w_key, w_value, w_out, c_query, c_key, c_value, c_out, f_in, f_out = gathered
    local_memory = memory.reshape(-1, feat_width)
    local_keys = matmul(local_memory, c_key).astype(bf16).reshape(memory.shape)
    local_values = matmul(local_memory, c_value).astype(bf16).reshape(memory.shape)
    cross_keys, cross_values = (
        lax.all_to_all(local_keys, "mem", split_axis=0, concat_axis=1, tiled=True),
        lax.all_to_all(local_values, "mem", split_axis=0, concat_axis=1, tiled=True),
    )
    signal_low = step_signal(timesteps, feat_width).astype(bf16)
    embedded = matmul(signal_low, w_time)
    resid = (decoder_input.astype(jnp.float32) + embedded[:, None, :]).reshape(
        row_count, feat_width
    )
    gain_one = norm_gains[:, 0]
    gain_two = norm_gains[:, 1]
    gain_three = norm_gains[:, 2]
    normed_one = layer_norm(resid, gain_one).astype(bf16)
    queries = matmul(normed_one, w_query).astype(bf16)
    keys = matmul(normed_one, w_key).astype(bf16)
    values = matmul(normed_one, w_value).astype(bf16)
    self_keys = keys.reshape(seg_count, seg_len, feat_width)
    self_values = values.reshape(seg_count, seg_len, feat_width)
    attended, self_totals = attend_segments(queries, self_keys, self_values, HEADS)
    mid = resid + matmul(attended, w_out)
    normed_two = layer_norm(mid, gain_two).astype(bf16)
    cross_q = matmul(normed_two, c_query).astype(bf16)
    crossed, cross_totals = attend_segments(cross_q, cross_keys, cross_values, HEADS)
    late = mid + matmul(crossed, c_out)
    normed_three = layer_norm(late, gain_three).astype(bf16)
    first_inner = matmul(normed_three, f_in)
    first_active = jax.nn.gelu(first_inner, approximate=False).astype(bf16)
    layer_output = (late + matmul(first_active, f_out)).astype(bf16).reshape(decoder_input.shape)
    branch_three = cotangent.reshape(row_count, feat_width)
    inner = matmul(normed_three, f_in)
    active, gelu_pull = jax.vjp(lambda pre_act: jax.nn.gelu(pre_act, approximate=False), inner)
    raw_ffn_out = matmul_tn(active.astype(bf16), branch_three)
    grad_active = matmul_nt(branch_three, f_out)
    grad_inner = gelu_pull(grad_active)[0].astype(bf16)
    raw_ffn_in = matmul_tn(normed_three, grad_inner)
    _, norm_pull = jax.vjp(layer_norm, late, gain_three)
    late_part, raw_gain_three = norm_pull(matmul_nt(grad_inner, f_in))
    grad_late = branch_three.astype(jnp.float32) + late_part
    branch_two = grad_late.astype(bf16)
    raw_cross_out = matmul_tn(crossed, branch_two)
    grad_crossed = matmul_nt(branch_two, c_out).astype(bf16)
    grad_cross_q, grad_cross_keys, grad_cross_values = attend_segments_back(
        cross_q, cross_keys, cross_values, cross_totals, grad_crossed, HEADS
    )
    raw_cross_query = matmul_tn(normed_two, grad_cross_q)
    back_keys, back_values = (
        lax.all_to_all(grad_cross_keys, "mem", split_axis=1, concat_axis=0, tiled=True),
        lax.all_to_all(grad_cross_values, "mem", split_axis=1, concat_axis=0, tiled=True),
    )
    flat_keys = back_keys.reshape(-1, feat_width)
    flat_values = back_values.reshape(-1, feat_width)
    raw_cross_key = matmul_tn(local_memory, flat_keys)
    raw_cross_value = matmul_tn(local_memory, flat_values)
    memory_grad = (
        (matmul_nt(flat_keys, c_key) + matmul_nt(flat_values, c_value))
        .astype(bf16)
        .reshape(memory.shape)
    )
    _, norm_pull = jax.vjp(layer_norm, mid, gain_two)
    mid_part, raw_gain_two = norm_pull(matmul_nt(grad_cross_q, c_query))
    grad_mid = grad_late + mid_part
    branch_one = grad_mid.astype(bf16)
    raw_attn_out = matmul_tn(attended, branch_one)
    grad_attended = matmul_nt(branch_one, w_out).astype(bf16)
    grad_queries, grad_keys, grad_values = attend_segments_back(
        queries, self_keys, self_values, self_totals, grad_attended, HEADS
    )
    grad_keys = grad_keys.reshape(row_count, feat_width)
    grad_values = grad_values.reshape(row_count, feat_width)
    raw_attn_query = matmul_tn(normed_one, grad_queries)
    raw_attn_key = matmul_tn(normed_one, grad_keys)
    raw_attn_value = matmul_tn(normed_one, grad_values)
    grad_normed = (
        matmul_nt(grad_queries, w_query)
        + matmul_nt(grad_keys, w_key)
        + matmul_nt(grad_values, w_value)
    )
    _, norm_pull = jax.vjp(layer_norm, resid, gain_one)
    resid_part, raw_gain_one = norm_pull(grad_normed)
    grad_resid = grad_mid + resid_part
    input_grad = grad_resid.astype(bf16).reshape(decoder_input.shape)
    segment_sums = jnp.sum(grad_resid.reshape(seg_count, seg_len, feat_width), axis=1)
    raw_time = jnp.dot(
        signal_low.astype(jnp.float32).T, segment_sums, precision=lax.Precision.HIGHEST
    )
    gain_partial = jnp.stack([raw_gain_one, raw_gain_two, raw_gain_three], axis=1)
    mem_count = lax.axis_size("mem")
    weight_partial = (
        raw_time,
        raw_attn_query,
        raw_attn_key,
        raw_attn_value,
        raw_attn_out,
        raw_cross_query,
        raw_cross_key,
        raw_cross_value,
        raw_cross_out,
        raw_ffn_in,
        raw_ffn_out,
    )
    wide_done = lax.psum_scatter(
        weight_partial + (gain_partial,), "dp", scatter_dimension=0, tiled=True
    )
    summed = jax.tree.map(
        lambda part: part.astype(jnp.float32),
        lax.psum_scatter(
            shortened(wide_done[:-1] + (jnp.tile(wide_done[-1], (1, mem_count)),)),
            "mem",
            scatter_dimension=1,
            tiled=True,
        ),
    )
    weight_done = summed[:-1]
    gains_done = summed[-1]
    local_squares = jnp.sum(gains_done * gains_done) / mem_count
    for grad_item in weight_done:
        local_squares = local_squares + jnp.sum(grad_item * grad_item)
    total_squares = lax.psum(local_squares, ("dp", "mem"))
    limit = math.sqrt(9 * D * D + 2 * D * FF + 3 * D)
    factor = jnp.minimum(1.0, limit * lax.rsqrt(total_squares))
    clipped = tuple((grad_item * factor for grad_item in weight_done))
    return (
        layer_output,
        input_grad,
        memory_grad,
        clipped[0],
        clipped[1],
        clipped[2],
        clipped[3],
        clipped[4],
        clipped[5],
        clipped[6],
        clipped[7],
        clipped[8],
        clipped[9],
        clipped[10],
        gains_done * factor,
    )


def solution(mesh):
    in_specs = (
        P(("dp", "mem"), None, None),
        P(("dp", "mem")),
        P("dp", "mem", None),
        P(("dp", "mem"), None, None),
        P("dp", None),
        P("dp", None),
        P("dp", None),
        P("dp", None),
        P("dp", None),
        P("dp", None),
        P("dp", None),
        P("dp", None),
        P("dp", None),
        P("dp", None),
        P("dp", None),
        P(),
    )
    out_specs = (
        P(("dp", "mem"), None, None),
        P(("dp", "mem"), None, None),
        P("dp", "mem", None),
        P("dp", "mem"),
        P("dp", "mem"),
        P("dp", "mem"),
        P("dp", "mem"),
        P("dp", "mem"),
        P("dp", "mem"),
        P("dp", "mem"),
        P("dp", "mem"),
        P("dp", "mem"),
        P("dp", "mem"),
        P("dp", "mem"),
        P("dp", None),
    )
    return jax.shard_map(
        per_device, mesh=mesh, in_specs=in_specs, out_specs=out_specs, check_vma=False
    )
```

profile of v0, /device:TPU:12, one launch (start us, length us, event | category | flops | bytes accessed | tf_op | source)
XLA Modules:
  0.0 1081.1 jit_solution(7287212211221837603)
XLA Ops:
  27.7 11.2 %all_gather.35 = bf16[512,512]{1,0:T(8,128)(2,1)S(1)} all-gather(bf16[64,512]{1,0:T(8,128)(2,1)S(1)} %copy-done.79), channel_id=1, replica_groups=mesh['dp'=8,'mem'=4] {'dp'}, dimensions={0}, use_global_device_ids=true | all-gather | bytes 589824 | tf_op jit(solution)/shard_map/all_gather | solution.py:163
  38.9 10.5 all_gather.36
  59.2 13.2 %all_gather.33 = bf16[512,512]{1,0:T(8,128)(2,1)} all-gather(bf16[64,512]{1,0:T(8,128)(2,1)S(1)} %copy-done.82), channel_id=1, replica_groups=mesh['dp'=8,'mem'=4] {'dp'}, dimensions={0}, use_global_device_ids=true | all-gather | bytes 589824 | tf_op jit(solution)/shard_map/all_gather | solution.py:162
  126.2 10.6 all_gather.39
  155.3 10.6 all_gather.41
  212.3 24.7 %multiply_convert_fusion.4 = (bf16[1024,2048]{1,0:T(8,128)(2,1)}, f32[1024,2048]{1,0:T(8,128)}, f32[1024,2048]{1,0:T(8,128)}) fusion(bf16[512,2048]{1,0:T(8,128)(2,1)} %all-gather.3.cloned.1.call-done, f32[1024,512]{0,1:T(8,128)} %copy-done.18, f32[512]{0:T(512)S(1)} %bitcast.334, f32[1024]{0:T(1024)S(1)} %fusion.85, f32[1024]{0:T(1024)S(1)} %broadcast_multiply_fusion.1), kind=kOutput, calls=%fused_computation.43 | convolution fusion | flops 2285895680 | bytes 25176064 | tf_op jit(solution)/shard_map/dot_general | solution.py:32
  257.2 16.3 %multiply_reduce_fusion.3 = (f32[8,512]{1,0:T(8,128)}, f32[8,512,1024]{2,1,0:T(8,128)}) fusion(f32[8,512,1024]{2,1,0:T(8,128)} %copy-done.3, f32[8,512]{1,0:T(8,128)S(1)} %log_add_fusion.3, bf16[512,8,64]{0,2,1:T(8,128)(2,1)S(1)} %bitcast.249, bf16[1024,8,64]{0,2,1:T(8,128)(2,1)S(1)} %copy-done.27), kind=kOutput, calls=%fused_computation.10 | convolution fusion | flops 553644032 | bytes 35160064 | tf_op jit(solution)/shard_map/qhd,khd->hqk/dot_general | solution.py:94
  273.5 10.6 multiply_convert_fusion.3
  291.1 15.0 %multiply_reduce_fusion.2 = (f32[8,512]{1,0:T(8,128)}, f32[8,512,1024]{2,1,0:T(8,128)}) fusion(f32[8,512,1024]{2,1,0:T(8,128)} %copy-done.4, f32[8,512]{1,0:T(8,128)S(1)} %copy-done.70, bf16[512,8,64]{0,2,1:T(8,128)(2,1)S(1)} %bitcast.251, bf16[1024,8,64]{0,2,1:T(8,128)(2,1)} %reshape_squeeze.8), kind=kOutput, calls=%fused_computation.7 | convolution fusion | flops 553644032 | bytes 35160064 | tf_op jit(solution)/shard_map/qhd,khd->hqk/dot_general | solution.py:94
  362.1 11.9 %multiply_reduce_fusion.1 = (f32[8,512]{1,0:T(8,128)S(1)}, f32[8,512,1024]{2,1,0:T(8,128)}) fusion(f32[8,512,1024]{2,1,0:T(8,128)} %get-tuple-element.132, f32[8,512]{1,0:T(8,128)S(1)} %copy-done.67, bf16[512,8,64]{0,2,1:T(8,128)(2,1)S(1)} %bitcast.256, bf16[1024,8,64]{0,2,1:T(8,128)(2,1)} %bitcast.263), kind=kOutput, calls=%fused_computation.4 | convolution fusion | flops 553644032 | bytes 35160064 | tf_op jit(solution)/shard_map/qhd,khd->hqk/dot_general | solution.py:94
  374.1 12.0 %multiply_convert_fusion.1 = bf16[8,512,1024]{2,1,0:T(8,128)(2,1)S(1)} fusion(f32[8,512,1024]{2,1,0:T(8,128)} %get-tuple-element.152, f32[8,512,1024]{2,1,0:T(8,128)} %get-tuple-element.132, f32[8,512]{1,0:T(8,128)S(1)} %get-tuple-element.151, f32[8,512]{1,0:T(8,128)S(1)} %copy-done.67), kind=kLoop, calls=%fused_computation.3 | loop fusion | flops 20971520 | bytes 41975808 | tf_op jit(solution)/shard_map/convert_element_type | solution.py:98
  392.3 11.5 %multiply_reduce_fusion = (f32[8,512]{1,0:T(8,128)S(1)}, f32[8,512,1024]{2,1,0:T(8,128)}) fusion(f32[8,512,1024]{2,1,0:T(8,128)} %copy-done.1, f32[8,512]{1,0:T(8,128)S(1)} %copy-done.66, bf16[512,8,64]{0,2,1:T(8,128)(2,1)S(1)} %bitcast.254, bf16[1024,8,64]{0,2,1:T(8,128)(2,1)S(1)} %bitcast.264), kind=kOutput, calls=%fused_computation.1 | convolution fusion | flops 553644032 | bytes 35160064 | tf_op jit(solution)/shard_map/qhd,khd->hqk/dot_general | solution.py:94
  403.9 12.9 %multiply_convert_fusion = bf16[8,512,1024]{2,1,0:T(8,128)(2,1)S(1)} fusion(f32[8,512,1024]{2,1,0:T(8,128)} %get-tuple-element.150, f32[8,512,1024]{2,1,0:T(8,128)} %copy-done.1, f32[8,512]{1,0:T(8,128)S(1)} %get-tuple-element.149, f32[8,512]{1,0:T(8,128)S(1)} %copy-done.66), kind=kLoop, calls=%fused_computation | loop fusion | flops 20971520 | bytes 41975808 | tf_op jit(solution)/shard_map/convert_element_type | solution.py:98
  422.8 11.0 %add_convert_fusion.2 = bf16[8,64,1024]{2,1,0:T(8,128)(2,1)} fusion(f32[8,64,1024]{2,1,0:T(8,128)} %fusion.12, bf16[512,8,64]{0,2,1:T(8,128)(2,1)} %bitcast.250, f32[8,512,1024]{2,1,0:T(8,128)} %copy-done.3, f32[8,512]{1,0:T(8,128)S(1)} %copy-done.69), kind=kOutput, calls=%fused_computation.75 | convolution fusion | flops 550502400 | bytes 20463616 | tf_op jit(solution)/shard_map/hqk,qhd->khd/dot_general | solution.py:99
  530.0 20.3 %all-to-all-done.2 = bf16[4,2,65536]{2,1,0:T(2,128)(2,1)} async-done(((bf16[4,2,65536]{2,1,0:T(2,128)(2,1)}), bf16[4,2,65536]{2,1,0:T(2,128)(2,1)}, u32[]{:S(2)}, u32[]{:S(2)}) %all-to-all-start.2) | async-done | bytes 1048608 | tf_op jit(solution)/shard_map/all_to_all | solution.py:224
  593.4 20.2 %reduce-scatter.88.cloned.1.call-done = f32[64,512]{1,0:T(8,128)} async-done(((f32[512,512]{1,0:T(8,128)}), f32[64,512]{1,0:T(8,128)}) %reduce-scatter.88.cloned.1.call-update) | async-done | bytes 131088 | tf_op jit(solution)/shard_map/reduce_scatter | solution.py:278
  626.1 24.2 %reduce-scatter.72.cloned.1.call-done = f32[64,3]{1,0:T(8,128)} async-done(((f32[512,3]{1,0:T(8,128)}), f32[64,3]{1,0:T(8,128)}) %reduce-scatter.72.cloned.1.call-update) | async-done | bytes 784
  661.4 28.3 %reduce-scatter.84.cloned.1.call-done = f32[64,512]{1,0:T(8,128)} async-done(((f32[512,512]{1,0:T(8,128)}), f32[64,512]{1,0:T(8,128)}) %reduce-scatter.84.cloned.1.call-update) | async-done | bytes 131088 | tf_op jit(solution)/shard_map/reduce_scatter | solution.py:278
  693.9 14.6 %reduce-scatter.92.cloned.1.call-done = bf16[128,64]{1,0:T(8,128)(2,1)} async-done(((bf16[512,64]{1,0:T(8,128)(2,1)}), bf16[128,64]{1,0:T(8,128)(2,1)}) %reduce-scatter.92.cloned.1.call-update) | async-done | bytes 16400
  709.3 18.6 %reduce-scatter.82.cloned.1.call-done = bf16[128,64]{1,0:T(8,128)(2,1)} async-done(((bf16[512,64]{1,0:T(8,128)(2,1)}), bf16[128,64]{1,0:T(8,128)(2,1)}) %reduce-scatter.82.cloned.1.call-update) | async-done | bytes 16400
  728.8 18.8 %reduce-scatter.80.cloned.1.call-done = bf16[128,64]{1,0:T(8,128)(2,1)} async-done(((bf16[512,64]{1,0:T(8,128)(2,1)}), bf16[128,64]{1,0:T(8,128)(2,1)}) %reduce-scatter.80.cloned.1.call-update) | async-done | bytes 16400
  748.4 18.6 %reduce-scatter.78.cloned.1.call-done = bf16[128,64]{1,0:T(8,128)(2,1)} async-done(((bf16[512,64]{1,0:T(8,128)(2,1)}), bf16[128,64]{1,0:T(8,128)(2,1)}) %reduce-scatter.78.cloned.1.call-update) | async-done | bytes 16400
  767.9 18.8 %reduce-scatter.76.cloned.1.call-done = bf16[128,64]{1,0:T(8,128)(2,1)} async-done(((bf16[512,64]{1,0:T(8,128)(2,1)}), bf16[128,64]{1,0:T(8,128)(2,1)}) %reduce-scatter.76.cloned.1.call-update) | async-done | bytes 16400
  787.5 19.2 %reduce-scatter.74.cloned.1.call-done = bf16[128,64]{1,0:T(8,128)(2,1)} async-done(((bf16[512,64]{1,0:T(8,128)(2,1)}), bf16[128,64]{1,0:T(8,128)(2,1)}) %reduce-scatter.74.cloned.1.call-update) | async-done | bytes 16400
  807.5 19.5 %reduce-scatter.70.cloned.1.call-done = bf16[128,64]{1,0:T(8,128)(2,1)} async-done(((bf16[512,64]{1,0:T(8,128)(2,1)}), bf16[128,64]{1,0:T(8,128)(2,1)}) %reduce-scatter.70.cloned.1.call-update) | async-done | bytes 16400
  827.8 54.6 %reduce-scatter.68.cloned.1.call-done = f32[256,512]{1,0:T(8,128)} async-done(((f32[2048,512]{1,0:T(8,128)}), f32[256,512]{1,0:T(8,128)}) %reduce-scatter.68.cloned.1.call-update) | async-done | bytes 524304 | tf_op jit(solution)/shard_map/reduce_scatter | solution.py:278
  890.7 46.8 %reduce-scatter.64.cloned.1.call-done = f32[64,2048]{1,0:T(8,128)} async-done(((f32[512,2048]{1,0:T(8,128)}), f32[64,2048]{1,0:T(8,128)}) %reduce-scatter.64.cloned.1.call-update) | async-done | bytes 524304 | tf_op jit(solution)/shard_map/reduce_scatter | solution.py:278
  941.2 15.1 %reduce-scatter.90.cloned.1.call-done = bf16[128,64]{1,0:T(8,128)(2,1)} async-done(((bf16[512,64]{1,0:T(8,128)(2,1)}), bf16[128,64]{1,0:T(8,128)(2,1)}) %reduce-scatter.90.cloned.1.call-update) | async-done | bytes 16400
  957.1 18.9 %reduce-scatter.86.cloned.1.call-done = bf16[128,64]{1,0:T(8,128)(2,1)} async-done(((bf16[512,64]{1,0:T(8,128)(2,1)}), bf16[128,64]{1,0:T(8,128)(2,1)}) %reduce-scatter.86.cloned.1.call-update) | async-done | bytes 16400
  980.0 15.8 %reduce-scatter.94.cloned.1.call-done = bf16[128,256]{1,0:T(8,128)(2,1)} async-done(((bf16[512,256]{1,0:T(8,128)(2,1)}), bf16[128,256]{1,0:T(8,128)(2,1)}) %reduce-scatter.94.cloned.1.call-update) | async-done | bytes 65552
  997.5 19.3 %reduce-scatter.66.cloned.1.call-done = bf16[64,512]{1,0:T(8,128)(2,1)} async-done(((bf16[64,2048]{1,0:T(8,128)(2,1)}), bf16[64,512]{1,0:T(8,128)(2,1)}) %reduce-scatter.66.cloned.1.call-update) | async-done | bytes 65552 | tf_op jit(solution)/shard_map/reduce_scatter | solution.py:283
  1023.0 43.1 %psum.7 = f32[]{:T(128)} all-reduce(f32[]{:T(128)S(6)} %add.233), channel_id=1, replica_groups=mesh['dp'=8,'mem'=4] {'dp','mem'}, use_global_device_ids=true, to_apply=%region_64.0 | all-reduce | flops 1 | bytes 8 | tf_op jit(solution)/shard_map/psum | solution.py:295
  (480 shorter events, 438.6 us)
Async XLA Ops:
  7.2 205.0 %all-gather.3.cloned.1.call-start = ((), (), s32[]{:S(2)}) async-start(), calls=%async_computation.27 | async-start | bytes 2359296 | tf_op jit(solution)/shard_map/all_gather | solution.py:171
  20.3 129.9 %all-to-all-start = ((bf16[4,256,512]{2,1,0:T(8,128)(2,1)}), bf16[4,256,512]{2,1,0:T(8,128)(2,1)}, u32[]{:S(2)}, u32[]{:S(2)}) async-start(bf16[4,256,512]{2,1,0:T(8,128)(2,1)} %bitcast.13), calls=%async_computation | async-start | bytes 2097152 | tf_op jit(solution)/shard_map/all_to_all | solution.py:180
  25.6 211.4 %all-gather.5.cloned.1.call-start = ((), (), s32[]{:S(2)}) async-start(), calls=%async_computation.28 | async-start | bytes 2359296 | tf_op jit(solution)/shard_map/all_gather | solution.py:172
  27.7 139.7 %copy-start.97 = (f32[512,1]{0,1:T(1,128)}, f32[512,1]{0,1:T(1,128)S(1)}, u32[]{:S(2)}) copy-start(f32[512,1]{0,1:T(1,128)S(1)} %get-tuple-element.126) | copy-start | bytes 6148
  27.7 221.5 %copy-start.104 = (f32[512,1]{0,1:T(1,128)}, f32[512,1]{0,1:T(1,128)S(1)}, u32[]{:S(2)}) copy-start(f32[512,1]{0,1:T(1,128)S(1)} %get-tuple-element.124) | copy-start | bytes 6148
  75.5 70.4 %copy-start.77 = (f32[1,512]{1,0:T(1,128)}, f32[1,512]{1,0:T(1,128)S(1)}, u32[]{:S(2)}) copy-start(f32[1,512]{1,0:T(1,128)S(1)} %fusion.121) | copy-start | bytes 6148
  150.2 28.1 %all-to-all-start.1 = ((bf16[4,256,512]{2,1,0:T(8,128)(2,1)}), bf16[4,256,512]{2,1,0:T(8,128)(2,1)}, u32[]{:S(2)}, u32[]{:S(2)}) async-start(bf16[4,256,512]{2,1,0:T(8,128)(2,1)} %bitcast.276), calls=%async_computation.1 | async-start | bytes 2097152 | tf_op jit(solution)/shard_map/all_to_all | solution.py:179
  155.3 402.3 %reduce-scatter.62.cloned.1.call-start = ((), (), s32[]{:S(2)}) async-start(), calls=%async_computation.35 | async-start | bytes 1179648 | tf_op jit(solution)/shard_map/reduce_scatter | solution.py:278
  257.1 302.2 %reduce-scatter.60.cloned.1.call-start = ((), (), s32[]{:S(2)}) async-start(), calls=%async_computation.34 | async-start | bytes 1179648 | tf_op jit(solution)/shard_map/reduce_scatter | solution.py:278
  340.3 220.8 %reduce-scatter.58.cloned.1.call-start = ((), (), s32[]{:S(2)}) async-start(), calls=%async_computation.33 | async-start | bytes 1179648 | tf_op jit(solution)/shard_map/reduce_scatter | solution.py:278
  374.0 188.8 %reduce-scatter.56.cloned.1.call-start = ((), (), s32[]{:S(2)}) async-start(), calls=%async_computation.32 | async-start | bytes 1179648 | tf_op jit(solution)/shard_map/reduce_scatter | solution.py:278
  403.9 160.7 %reduce-scatter.54.cloned.1.call-start = ((), (), s32[]{:S(2)}) async-start(), calls=%async_computation.31 | async-start | bytes 1179648 | tf_op jit(solution)/shard_map/reduce_scatter | solution.py:278
  460.2 56.8 %all-to-all-start.3 = ((bf16[4,2,65536]{2,1,0:T(2,128)(2,1)}), bf16[4,2,65536]{2,1,0:T(2,128)(2,1)}, u32[]{:S(2)}, u32[]{:S(2)}) async-start(bf16[4,2,65536]{2,1,0:T(2,128)(2,1)} %reshape.437), calls=%async_computation.3 | async-start | bytes 2097152 | tf_op jit(solution)/shard_map/all_to_all | solution.py:225
  468.0 98.4 %reduce-scatter.52.cloned.1.call-start = ((), (), s32[]{:S(2)}) async-start(), calls=%async_computation.30 | async-start | bytes 1179648 | tf_op jit(solution)/shard_map/reduce_scatter | solution.py:278
  481.3 93.2 %reduce-scatter.50.cloned.1.call-start = ((), (), s32[]{:S(2)}) async-start(), calls=%async_computation.29 | async-start | bytes 1179648 | tf_op jit(solution)/shard_map/reduce_scatter | solution.py:278
  489.4 124.3 %reduce-scatter.88.cloned.1.call-start = ((), (), s32[]{:S(2)}) async-start(), calls=%async_computation.48 | async-start | bytes 1179648 | tf_op jit(solution)/shard_map/reduce_scatter | solution.py:278
  524.0 26.3 %all-to-all-start.2 = ((bf16[4,2,65536]{2,1,0:T(2,128)(2,1)}), bf16[4,2,65536]{2,1,0:T(2,128)(2,1)}, u32[]{:S(2)}, u32[]{:S(2)}) async-start(bf16[4,2,65536]{2,1,0:T(2,128)(2,1)} %reshape.435), calls=%async_computation.2 | async-start | bytes 2097152 | tf_op jit(solution)/shard_map/all_to_all | solution.py:224
  529.1 121.3 %reduce-scatter.72.cloned.1.call-start = ((), (), s32[]{:S(2)}) async-start(), calls=%async_computation.40 | async-start | bytes 294912
  530.0 159.7 %reduce-scatter.84.cloned.1.call-start = ((), (), s32[]{:S(2)}) async-start(), calls=%async_computation.46 | async-start | bytes 1179648 | tf_op jit(solution)/shard_map/reduce_scatter | solution.py:278
  557.2 151.2 %reduce-scatter.92.cloned.1.call-start = ((), (), s32[]{:S(2)}) async-start(), calls=%async_computation.50 | async-start | bytes 163840
  559.2 168.7 %reduce-scatter.82.cloned.1.call-start = ((), (), s32[]{:S(2)}) async-start(), calls=%async_computation.45 | async-start | bytes 163840
  561.0 186.6 %reduce-scatter.80.cloned.1.call-start = ((), (), s32[]{:S(2)}) async-start(), calls=%async_computation.44 | async-start | bytes 163840
  562.8 204.3 %reduce-scatter.78.cloned.1.call-start = ((), (), s32[]{:S(2)}) async-start(), calls=%async_computation.43 | async-start | bytes 163840
  564.5 222.1 %reduce-scatter.76.cloned.1.call-start = ((), (), s32[]{:S(2)}) async-start(), calls=%async_computation.42 | async-start | bytes 163840
  566.3 240.4 %reduce-scatter.74.cloned.1.call-start = ((), (), s32[]{:S(2)}) async-start(), calls=%async_computation.41 | async-start | bytes 163840
  568.1 258.9 %reduce-scatter.70.cloned.1.call-start = ((), (), s32[]{:S(2)}) async-start(), calls=%async_computation.39 | async-start | bytes 163840
  576.3 306.2 %reduce-scatter.68.cloned.1.call-start = ((), (), s32[]{:S(2)}) async-start(), calls=%async_computation.38 | async-start | bytes 4718592 | tf_op jit(solution)/shard_map/reduce_scatter | solution.py:278
  583.2 354.3 %reduce-scatter.64.cloned.1.call-start = ((), (), s32[]{:S(2)}) async-start(), calls=%async_computation.36 | async-start | bytes 4718592 | tf_op jit(solution)/shard_map/reduce_scatter | solution.py:278
  591.5 364.7 %reduce-scatter.90.cloned.1.call-start = ((), (), s32[]{:S(2)}) async-start(), calls=%async_computation.49 | async-start | bytes 163840
  615.3 360.7 %reduce-scatter.86.cloned.1.call-start = ((), (), s32[]{:S(2)}) async-start(), calls=%async_computation.47 | async-start | bytes 163840
  691.4 304.5 %reduce-scatter.94.cloned.1.call-start = ((), (), s32[]{:S(2)}) async-start(), calls=%async_computation.51 | async-start | bytes 327680
  884.4 132.4 %reduce-scatter.66.cloned.1.call-start = ((), (), s32[]{:S(2)}) async-start(), calls=%async_computation.37 | async-start | bytes 327680 | tf_op jit(solution)/shard_map/reduce_scatter | solution.py:283
  (116 other events, 1282.5 us)
Sparse Core Ops, SparseCore 0:
  10.0 30.6 all-gather.2
  42.6 30.7 all-gather.4
  257.2 37.6 reduce-scatter.61
  340.4 37.7 reduce-scatter.59
  381.2 36.0 reduce-scatter.57
  420.3 35.9 reduce-scatter.55
  459.5 36.0 reduce-scatter.53
  498.7 35.9 reduce-scatter.51
  538.5 35.9 reduce-scatter.49
  577.6 35.9 reduce-scatter.87
  616.7 33.6 reduce-scatter.71
  653.7 35.9 reduce-scatter.83
  692.0 16.4 reduce-scatter.91
  710.6 17.3 reduce-scatter.81
  730.1 17.3 reduce-scatter.79
  749.7 17.3 reduce-scatter.77
  769.2 17.3 reduce-scatter.75
  789.3 17.3 reduce-scatter.73
  809.6 17.3 reduce-scatter.69
  830.2 52.2 reduce-scatter.67
  886.2 51.2 reduce-scatter.63
  939.8 16.4 reduce-scatter.89
  958.6 17.3 reduce-scatter.85
  978.1 17.7 reduce-scatter.93
  998.8 17.9 reduce-scatter.65
where the time goes:
time: 1090 us; the launch traced here: 1080 us
  waiting for transfers between devices  403 us (37%)
  matrix products  273 us (25%)
  blocking collectives  146 us (13%)
  other arithmetic  119 us (11%)
  local copies, waits for them, and re-layouts  89.1 us (8%)
  between operations  25.8 us (2%)
  starting transfers between devices  24.5 us (2%)
    unnamed x36, waiting for transfers between devices  204 us
    reduce_scatter x11, waiting for transfers between devices, per_device(): lax.psum_scatter(weight_partial + (gain_partial,), 'dp', scatter_dimensio...  157 us
    unnamed x272, local copies, waits for them, and re-layouts  66.2 us
    dot_general x4, matrix products, attend_backward(): jnp.einsum('qhd,khd->hqk', grad_heads, value_heads, preferred_element_typ...  54.7 us
    convert_element_type x4, other arithmetic, attend_backward(): grad_scores = (probs_full * (grad_probs - row_inner)).astype(jnp.bfloat16)  45.9 us
    dot_general x11, matrix products, matmul(): return jnp.dot(first_op, second_op, preferred_element_type=jnp.float32)  44.8 us
    psum x1, blocking collectives, per_device(): total_squares = lax.psum(local_squares, ('dp', 'mem'))  43.1 us
    dot_general x4, matrix products, attend_backward(): jnp.einsum('hqk,qhd->khd', probs_full.astype(jnp.bfloat16), grad_heads, p...  36.7 us
  transfers between devices with their start and end apart: 29, of which 19 were waited for; matrix products, arithmetic and copies ran while one was open for 40% of the time, Pallas kernels for 0%

commit v1 on v0

v1 whole, which is shorter than its diff:
```python
import functools
import math

import jax
import jax.numpy as jnp
from jax import lax
from jax.experimental import pallas as pl
from jax.experimental.pallas import tpu as pltpu
from jax.sharding import PartitionSpec as P

D = 512
HEADS = 8
HEAD = 64
FF = 2048
PAIRS = HEADS // 2
PAIR = 2 * HEAD
CHUNKS = FF // D
BF = jnp.bfloat16
F32 = jnp.float32
SCALE = 1.0 / math.sqrt(HEAD)
ROOT_HALF = math.sqrt(0.5)
BELL = 1.0 / math.sqrt(2.0 * math.pi)


def dot(a, b, ca=1, cb=0):
    return lax.dot_general(a, b, (((ca,), (cb,)), ((), ())), preferred_element_type=F32)


def row_mean(v):
    return jnp.sum(v, axis=-1, keepdims=True) * (1.0 / v.shape[-1])


def norm_parts(v):
    centred = v - row_mean(v)
    scale = lax.rsqrt(row_mean(centred * centred) + 1e-05)
    return centred * scale, scale


def norm_back(v, gain, grad):
    normed, scale = norm_parts(v)
    c = grad * gain
    gain_part = jnp.sum(grad * normed, axis=0, keepdims=True)
    return scale * (c - row_mean(c) - normed * row_mean(c * normed)), gain_part


def build(dst, src, which, me):
    blocks, _, rows, _ = src.shape
    for b in range(blocks):
        dst[rows * b : rows * (b + 1), :] = src[b ^ me, which]


def put(ref, at, mat):
    mat = mat.astype(ref.dtype)
    if len(ref.shape) == 3:
        ref[at] = mat
        return
    rb, cb, _, cols = ref.shape
    rows = D // rb
    for a in range(rb):
        for j in range(cb):
            ref[a, j, rows * at : rows * (at + 1), :] = mat[
                rows * a : rows * (a + 1), cols * j : cols * (j + 1)
            ]


def attend(i, qT, k, vT, oT, lse):
    n = qT.shape[2]
    row = lax.broadcasted_iota(jnp.int32, (PAIR, n), 0)
    zero = jnp.zeros((), BF)
    scores = []
    for h in range(2):
        mine = jnp.where((row // HEAD) == h, qT[i], zero)
        scores.append(dot(k[i], mine))
    for h in range(2):
        top = jnp.max(scores[h], axis=0, keepdims=True)
        e = jnp.exp(scores[h] - top)
        total = jnp.sum(e, axis=0, keepdims=True)
        out = dot(vT[i, HEAD * h : HEAD * (h + 1), :], e.astype(BF))
        oT[i, HEAD * h : HEAD * (h + 1), :] = (out * (1.0 / total)).astype(BF)
        lse[0, h : h + 1, :] = top + jnp.log(total)


def attend_back(i, q, qT, k, kT, v, g, gT, lse, delta, dqT, dk, dv):
    n = qT.shape[2]
    block = min(n, 512)
    row = lax.broadcasted_iota(jnp.int32, (PAIR, block), 0)
    lane = lax.broadcasted_iota(jnp.int32, (block, PAIR), 1)
    zero = jnp.zeros((), BF)
    acc_k = acc_v = None
    for j in range(n // block):
        at = slice(j * block, (j + 1) * block)
        for h in range(2):
            mine = jnp.where((row // HEAD) == h, qT[i, :, at], zero)
            s = dot(k[i], mine)
            dp = dot(v[i], jnp.where((row // HEAD) == h, gT[i, :, at], zero))
            p = jnp.exp(s - lse[0, h : h + 1, at])
            ds = (p * (dp - delta[i, h : h + 1, at])).astype(BF)
            one_v = dot(p.astype(BF), jnp.where((lane // HEAD) == h, g[i, at, :], zero))
            one_k = dot(ds, jnp.where((lane // HEAD) == h, q[i, at, :], zero))
            own = slice(HEAD * h, HEAD * (h + 1))
            dqT[i, own, at] = (dot(kT[i, own, :], ds) * SCALE).astype(BF)
            acc_v = one_v if acc_v is None else acc_v + one_v
            acc_k = one_k if acc_k is None else acc_k + one_k
    dk[i] = (acc_k * SCALE).astype(BF)
    dv[i] = acc_v.astype(BF)


def pairs_in(dst, src):
    for p in range(PAIRS):
        dst[p] = src[:, PAIR * p : PAIR * (p + 1)]


def pairs_in_T(dst, src, scale=None):
    for p in range(PAIRS):
        t = src[:, PAIR * p : PAIR * (p + 1)].T
        dst[p] = t if scale is None else t * jnp.asarray(scale, BF)


def from_pairs(src):
    return jnp.concatenate([src[p] for p in range(PAIRS)], axis=1)


def from_pairs_T(src):
    return jnp.concatenate([src[p].T for p in range(PAIRS)], axis=1)


def self_forward(me, x, emb, gains, g1, g2, n1, q, k, v, lse, att, mid, n2, cq, w, qs, ks, vs, qT, vT, oT):
    i = pl.program_id(0)

    @pl.when(i == 0)
    def _():
        resid = x[...].astype(F32) + emb[...]
        normed = (norm_parts(resid)[0] * gains[0:1, :]).astype(BF)
        n1[...] = normed
        for t, dst in ((1, qs), (2, ks), (3, vs)):
            build(w, g1, t, me[0])
            pairs_in(dst, dot(normed, w[...]).astype(BF))
        for p in range(PAIRS):
            qT[p] = qs[p].T * jnp.asarray(SCALE, BF)
            vT[p] = vs[p].T

    attend(i, qT, ks, vT, oT, lse)
    q[...] = qs[i]
    k[...] = ks[i]
    v[...] = vs[i]

    @pl.when(i == PAIRS - 1)
    def _():
        joined = from_pairs_T(oT)
        att[...] = joined
        build(w, g2, 0, me[0])
        new = x[...].astype(F32) + emb[...] + dot(joined, w[...])
        mid[...] = new
        normed = (norm_parts(new)[0] * gains[1:2, :]).astype(BF)
        n2[...] = normed
        build(w, g2, 1, me[0])
        cq[...] = dot(normed, w[...]).astype(BF)


def cross_forward(me, mem, cq, mid, gains, g2, k, v, lse, crossed, late, n3, w, ks, vs, qT, vT, oT):
    i = pl.program_id(0)

    @pl.when(i == 0)
    def _():
        for t, dst in ((2, ks), (3, vs)):
            build(w, g2, t, me[0])
            pairs_in(dst, dot(mem[...], w[...]).astype(BF))
        pairs_in_T(qT, cq, SCALE)
        for p in range(PAIRS):
            vT[p] = vs[p].T

    attend(i, qT, ks, vT, oT, lse)
    k[...] = ks[i]
    v[...] = vs[i]

    @pl.when(i == PAIRS - 1)
    def _():
        joined = from_pairs_T(oT)
        crossed[...] = joined
        build(w, g2, 4, me[0])
        new = mid[...] + dot(joined, w[...])
        late[...] = new
        n3[...] = (norm_parts(new)[0] * gains[2:3, :]).astype(BF)


def feed_forward(me, n3, late, cot, gains, g3, out, gl, bt, gain3, raw, win, wout, n3T, acc, gacc):
    i = pl.program_id(0)
    blocks, _, rows, _ = g3.shape

    @pl.when(i == 0)
    def _():
        n3T[...] = n3[...].T
        acc[...] = late[...]
        gacc[...] = jnp.zeros_like(gacc)

    build(win, g3, i, me[0])
    if blocks == 1:
        wout[...] = g3[0, CHUNKS + i]
    else:
        each = blocks // CHUNKS
        for u in range(each):
            for t in range(CHUNKS):
                lo = rows * (CHUNKS * u + t)
                wout[lo : lo + rows, :] = g3[(each * i + u) ^ me[0], CHUNKS + t]
    inner = dot(n3[...], win[...])
    share = 0.5 * (1.0 + lax.erf(inner * ROOT_HALF))
    active = (inner * share).astype(BF)
    acc[...] += dot(active, wout[...])
    grad_active = dot(cot[...], wout[...], 1, 1)
    slope = share + inner * (jnp.exp(-0.5 * inner * inner) * BELL)
    grad_inner = (slope * grad_active).astype(BF)
    raw_out = dot(active, cot[...], 0, 0).astype(BF)
    raw_in = dot(n3T[...], grad_inner).astype(BF)
    gacc[...] += dot(grad_inner, win[...], 1, 1)
    if blocks == 1:
        raw[i] = raw_in
        raw[CHUNKS + i] = raw_out
    else:
        cols = D // CHUNKS
        for a in range(blocks):
            for t in range(CHUNKS):
                raw[a, i, rows * t : rows * (t + 1), :] = raw_in[
                    rows * a : rows * (a + 1), cols * t : cols * (t + 1)
                ]
        tall = D // each
        for u in range(each):
            for j in range(CHUNKS):
                raw[each * i + u, j, tall : 2 * tall, :] = raw_out[
                    tall * u : tall * (u + 1), cols * j : cols * (j + 1)
                ]

    @pl.when(i == CHUNKS - 1)
    def _():
        out[...] = acc[...].astype(BF)
        part, gain_part = norm_back(late[...], gains[2:3, :], gacc[...])
        gain3[...] = gain_part
        total = cot[...].astype(F32) + part
        gl[...] = total
        bt[...] = total.astype(BF)


def start_back(branch, weight, joined, g, gT, delta):
    grad = dot(branch, weight, 1, 1).astype(BF)
    pairs_in(g, grad)
    for p in range(PAIRS):
        gT[p] = g[p].T
        other = joined[:, PAIR * p : PAIR * (p + 1)].T
        both = gT[p].astype(F32) * other.astype(F32)
        for h in range(2):
            delta[p, h : h + 1, :] = jnp.sum(both[HEAD * h : HEAD * (h + 1), :], axis=0, keepdims=True)


def cross_back(
    me, bt, gl, crossed, cq, k, v, lse, mem, n2, mid, gains, g2, att,
    raw, mem_grad, gm, b1, gain2,
    w, q, qT, ks, kT, vs, g, gT, delta, dqT, dk, dv,
):
    i = pl.program_id(0)

    @pl.when(i == 0)
    def _():
        build(w, g2, 4, me[0])
        start_back(bt[...], w[...], crossed, g, gT, delta)
        put(raw, 0, dot(crossed[...].T, bt[...]))
        pairs_in(q, cq)
        pairs_in_T(qT, cq, SCALE)
        pairs_in(ks, k)
        pairs_in_T(kT, k)
        pairs_in(vs, v)

    attend_back(i, q, qT, ks, kT, vs, g, gT, lse, delta, dqT, dk, dv)

    @pl.when(i == PAIRS - 1)
    def _():
        grad_q = from_pairs_T(dqT)
        grad_k = from_pairs(dk)
        grad_v = from_pairs(dv)
        put(raw, 1, dot(n2[...].T, grad_q))
        mT = mem[...].T
        put(raw, 2, dot(mT, grad_k))
        put(raw, 3, dot(mT, grad_v))
        build(w, g2, 1, me[0])
        part, gain_part = norm_back(mid[...], gains[1:2, :], dot(grad_q, w[...], 1, 1))
        gain2[...] = gain_part
        total = gl[...] + part
        gm[...] = total
        low = total.astype(BF)
        b1[...] = low
        put(raw, 4, dot(att[...].T, low))
        build(w, g2, 2, me[0])
        back = dot(grad_k, w[...], 1, 1)
        build(w, g2, 3, me[0])
        mem_grad[...] = (back + dot(grad_v, w[...], 1, 1)).astype(BF)


def self_back(
    me, b1, att, qn, k, v, lse, n1, g1, g2,
    raw, gn,
    w, q, qT, ks, kT, vs, g, gT, delta, dqT, dk, dv,
):
    i = pl.program_id(0)

    @pl.when(i == 0)
    def _():
        build(w, g2, 0, me[0])
        start_back(b1[...], w[...], att, g, gT, delta)
        pairs_in(q, qn)
        pairs_in_T(qT, qn, SCALE)
        pairs_in(ks, k)
        pairs_in_T(kT, k)
        pairs_in(vs, v)

    attend_back(i, q, qT, ks, kT, vs, g, gT, lse, delta, dqT, dk, dv)

    @pl.when(i == PAIRS - 1)
    def _():
        nT = n1[...].T
        grads = (from_pairs_T(dqT), from_pairs(dk), from_pairs(dv))
        for t in range(3):
            put(raw, t, dot(nT, grads[t]))
        total = None
        for t in range(3):
            build(w, g1, t + 1, me[0])
            one = dot(grads[t], w[...], 1, 1)
            total = one if total is None else total + one
        gn[...] = total


def finish_back(x, emb, gm, gn, gains, grad, sums):
    part, gain_part = norm_back(x[...].astype(F32) + emb[...], gains[0:1, :], gn[...])
    total = gm[...] + part
    grad[...] = total.astype(BF)
    sums[0:1, :] = jnp.sum(total, axis=0, keepdims=True)
    sums[1:2, :] = gain_part


def full(shape):
    return pl.BlockSpec(shape, lambda i: (0,) * len(shape))


def call(body, name, args, outs, scratch, steps, flops, limit=48):
    in_specs = [pl.BlockSpec(memory_space=pltpu.SMEM)]
    arrays = [args[0]]
    for a in args[1:]:
        if isinstance(a, tuple):
            arrays.append(a[0])
            in_specs.append(a[1])
        else:
            arrays.append(a)
            in_specs.append(full(a.shape))
    size = sum(math.prod(a.shape) * a.dtype.itemsize for a in arrays)
    size += sum(math.prod(s) * jnp.dtype(t).itemsize for s, t, _ in outs)
    return pl.pallas_call(
        body,
        grid=(steps,),
        in_specs=in_specs,
        out_specs=tuple(full(s) if b is None else b for s, _, b in outs),
        out_shape=tuple(jax.ShapeDtypeStruct(s, t) for s, t, _ in outs),
        scratch_shapes=scratch,
        compiler_params=pltpu.CompilerParams(vmem_limit_bytes=limit * 2**20),
        cost_estimate=pl.CostEstimate(flops=int(flops), bytes_accessed=size, transcendentals=0),
        name=name,
    )(*arrays)


def step_signal(step_ids, feat_width):
    half_width = feat_width // 2
    frequency = jnp.exp(-math.log(10000.0) * jnp.arange(half_width, dtype=F32) / half_width)
    angles = step_ids.astype(F32)[:, None] * frequency[None, :]
    return jnp.concatenate([jnp.sin(angles), jnp.cos(angles)], axis=1)


def segment_layer(me, x, emb, mem, cot, gains, g1, g2, g3, blocked):
    n = x.shape[0]
    r = mem.shape[0]
    nat = pl.BlockSpec((n, PAIR), lambda i: (0, i))
    nat_r = pl.BlockSpec((r, PAIR), lambda i: (0, i))
    rows2 = pl.BlockSpec((1, 2, n), lambda i: (i, 0, 0))
    wide = lambda m: pltpu.VMEM((PAIRS, m, PAIR), BF)
    tall = lambda m: pltpu.VMEM((PAIRS, PAIR, m), BF)
    weight = pltpu.VMEM((D, D), BF)
    proj = 2 * n * D * D * 1.5
    att = 2 * n * r * D * 5
    lse_out = ((PAIRS, 2, n), F32, rows2)
    n1, q, k, v, lse1, attended, mid, n2, cq = call(
        self_forward, "self_forward", (me, x, emb, gains, g1, g2),
        [((n, D), BF, None)] + [((n, D), BF, nat)] * 3
        + [lse_out, ((n, D), BF, None), ((n, D), F32, None), ((n, D), BF, None), ((n, D), BF, None)],
        [weight, wide(n), wide(n), wide(n), tall(n), tall(n), tall(n)],
        PAIRS, 5 * proj + 2 * att,
    )
    ck, cv, lse2, crossed, late, n3 = call(
        cross_forward, "cross_forward", (me, mem, cq, mid, gains, g2),
        [((r, D), BF, nat_r)] * 2 + [lse_out, ((n, D), BF, None), ((n, D), F32, None), ((n, D), BF, None)],
        [weight, wide(r), wide(r), tall(n), tall(r), tall(n)],
        PAIRS, 3 * proj + 2 * att,
    )

    def raw_shape(count):
        if blocked is None:
            return ((count, D, D), BF, None)
        dp, cols = blocked
        return ((dp, cols, count * D // dp, D // cols), BF, None)

    out, gl, bt, gain3, raw3 = call(
        feed_forward, "feed_forward", (me, n3, late, cot, gains, g3),
        [((n, D), BF, None), ((n, D), F32, None), ((n, D), BF, None), ((1, D), F32, None), raw_shape(2 * CHUNKS)],
        [weight, weight, pltpu.VMEM((D, n), BF), pltpu.VMEM((n, D), F32), pltpu.VMEM((n, D), F32)],
        CHUNKS, 24 * proj,
    )
    back_scratch = lambda m: [
        weight, wide(n), tall(n), wide(m), tall(m), wide(m), wide(n), tall(n),
        pltpu.VMEM((PAIRS, 2, n), F32), tall(n), wide(m), wide(m),
    ]
    raw2, mem_grad, gm, b1, gain2 = call(
        cross_back, "cross_back",
        (me, bt, gl, crossed, cq, ck, cv, (lse2, rows2), mem, n2, mid, gains, g2, attended),
        [raw_shape(5), ((r, D), BF, None), ((n, D), F32, None), ((n, D), BF, None), ((1, D), F32, None)],
        back_scratch(r), PAIRS, 9 * proj + 5 * att,
    )
    raw1, gn = call(
        self_back, "self_back",
        (me, b1, attended, q, k, v, (lse1, rows2), n1, g1, g2),
        [raw_shape(3), ((n, D), F32, None)],
        back_scratch(n), PAIRS, 7 * proj + 5 * att,
    )

    def last(me_ref, *refs):
        finish_back(*refs)

    input_grad, sums = call(
        last, "finish_back", (me, x, emb, gm, gn, gains),
        [((n, D), BF, None), ((2, D), F32, None)], [], 1, 100 * n * D,
    )
    return out, input_grad, mem_grad, (raw1, raw2, raw3), sums, gain2, gain3


def per_device(
    decoder_input, timesteps, memory, cotangent, time_weight, attn_query, attn_key, attn_value, attn_out,
    cross_query, cross_key, cross_value, cross_out, ffn_in, ffn_out, norm_gains,
):
    dp = lax.axis_size("dp")
    mem_count = lax.axis_size("mem")
    rows = D // dp
    blocked = (dp, mem_count) if rows % 16 == 0 and mem_count == CHUNKS and dp % CHUNKS == 0 else None

    def gather(parts):
        got = lax.all_gather(jnp.stack(parts, 0), "dp", axis=0, tiled=False)
        if blocked is None:
            got = got.transpose(1, 0, 2, 3).reshape(1, len(parts), D, D)
        return got

    g1 = gather((time_weight, attn_query, attn_key, attn_value))
    g2 = gather((attn_out, cross_query, cross_key, cross_value, cross_out))
    in_parts = [ffn_in[:, D * c : D * (c + 1)] for c in range(CHUNKS)]
    if blocked is None:
        whole_out = lax.all_gather(ffn_out, "dp", axis=0, tiled=True).reshape(1, CHUNKS, D, D)
        g3 = jnp.concatenate([gather(in_parts), whole_out], axis=1)
    else:
        g3 = gather(in_parts + [ffn_out[rows * c : rows * (c + 1)] for c in range(CHUNKS)])
    me = jnp.zeros((1,), jnp.int32)
    mem_rows = lax.all_to_all(memory, "mem", split_axis=0, concat_axis=1, tiled=True)[0]
    signal = step_signal(timesteps, D).astype(BF)
    w_time = g1[:, 0].reshape(D, D)
    emb = jnp.dot(signal, w_time, preferred_element_type=F32)
    out, input_grad, mem_grad, raws, sums, gain2, gain3 = segment_layer(
        me, decoder_input[0], emb, mem_rows, cotangent[0], norm_gains.T, g1, g2, g3, blocked
    )
    memory_grad = lax.all_to_all(mem_grad[None], "mem", split_axis=1, concat_axis=0, tiled=True)

    def scatter(raw):
        if blocked is None:
            count = raw.shape[0]
            part = lax.psum_scatter(raw, "dp", scatter_dimension=1, tiled=True)
            part = lax.psum_scatter(part, "mem", scatter_dimension=2, tiled=True)
            return [part[t].astype(F32) for t in range(count)]
        part = lax.psum_scatter(raw, "dp", scatter_dimension=0, tiled=False)
        part = lax.psum_scatter(part, "mem", scatter_dimension=0, tiled=False).astype(F32)
        return [part[rows * t : rows * (t + 1)] for t in range(part.shape[0] // rows)]

    if blocked is None:
        raw3 = raws[2]
        part = scatter(raw3[:CHUNKS].transpose(1, 0, 2).reshape(1, D, FF))
        ffn_in_grad = part[0]
        ffn_out_grad = scatter(raw3[CHUNKS:].reshape(1, FF, D))[0]
    else:
        part = scatter(raws[2])
        ffn_in_grad = jnp.concatenate(part[:CHUNKS], axis=1)
        ffn_out_grad = jnp.concatenate(part[CHUNKS:], axis=0)
    d_query, d_key, d_value = scatter(raws[0])
    d_cout, d_cquery, d_ckey, d_cvalue, d_out = scatter(raws[1])
    packed = jnp.concatenate([sums, gain2, gain3, signal.astype(F32)], axis=0)
    everyone = lax.all_gather(packed, ("dp", "mem"), axis=0, tiled=False)
    row0 = lax.axis_index("dp") * rows
    cols = D // mem_count
    col0 = lax.axis_index("mem") * cols
    my_signal = lax.dynamic_slice_in_dim(everyone[:, 4], row0, rows, axis=1)
    my_sums = lax.dynamic_slice_in_dim(everyone[:, 0], col0, cols, axis=1)
    d_time = jnp.dot(my_signal.T, my_sums, precision=lax.Precision.HIGHEST)
    all_gains = jnp.sum(everyone[:, 1:4], axis=0)
    d_gains = lax.dynamic_slice_in_dim(all_gains, row0, rows, axis=1).T
    weights = [
        d_time, d_query, d_key, d_value, d_out, d_cquery, d_ckey, d_cvalue, d_cout, ffn_in_grad, ffn_out_grad,
    ]
    local = sum(jnp.sum(w * w) for w in weights)
    squares = lax.psum(local, ("dp", "mem")) + jnp.sum(all_gains * all_gains)
    limit = math.sqrt(9 * D * D + 2 * D * FF + 3 * D)
    factor = jnp.minimum(1.0, limit * lax.rsqrt(squares))
    return (out[None], input_grad[None], memory_grad) + tuple(w * factor for w in weights) + (d_gains * factor,)


def solution(mesh):
    tokens = P(("dp", "mem"), None, None)
    weight = P("dp", None)
    in_specs = (tokens, P(("dp", "mem")), P("dp", "mem", None), tokens) + (weight,) * 11 + (P(),)
    out_specs = (tokens, tokens, P("dp", "mem", None)) + (P("dp", "mem"),) * 11 + (P("dp", None),)
    return jax.shard_map(per_device, mesh=mesh, in_specs=in_specs, out_specs=out_specs, check_vma=False)
```

time: 1090 us -> 496 us (0.46)
  matrix products: 273 us -> 1.01 us
  waiting for transfers between devices: 403 us -> 137 us
  Pallas kernels: 0 us -> 143 us
  other arithmetic: 119 us -> 19.8 us
  local copies, waits for them, and re-layouts: 89.1 us -> 32.9 us
  blocking collectives: 146 us -> 124 us
  starting transfers between devices: 24.5 us -> 10.9 us
    dot_general x55 -> x2, matrix products: 273 us -> 1.01 us  [the longest x1 0.84 us: per_device(): d_time = jnp.dot(my_signal.T, my_sums, precision=lax.Precision.HIGHEST)]
    unnamed x36 -> x9, waiting for transfers between devices: 204 us -> 1.17 us
    pallas_call x0 -> x6, Pallas kernels: none -> 143 us  [call(): pl.pallas_call(body, grid=(steps,), in_specs=in_specs, out_specs=tuple((f...]
    reduce_scatter x12 -> x6, waiting for transfers between devices: 176 us -> 89.8 us  [the longest x3 84 us: scatter(): part = lax.psum_scatter(raw, 'dp', scatter_dimension=0, tiled=False)]
    convert_element_type x16 -> x4, other arithmetic: 57.4 us -> 2.64 us  [the longest x3 2.63 us: scatter(): lax.psum_scatter(part, 'mem', scatter_dimension=0, tiled=False).astype(F32)]
    all_gather x2 -> x3, waiting for transfers between devices: 0.02 us -> 46.4 us  [gather(): got = lax.all_gather(jnp.stack(parts, 0), 'dp', axis=0, tiled=False)]
    unnamed x272 -> x67, local copies, waits for them, and re-layouts: 66.2 us -> 29.1 us
    reduce_sum x24 -> x6, other arithmetic: 32.1 us -> 3.2 us  [the longest x4 2.5 us: per_device(): local = sum((jnp.sum(w * w) for w in weights))]
  transfers between devices with their start and end apart: 29 -> 11, of which waited for: 19 -> 5; matrix products, arithmetic and copies ran while one was open for 40% -> 6% of each run, Pallas kernels for 0% -> 9%
where the time goes in v1:
time: 496 us; the launch traced here: 492 us
  Pallas kernels  143 us (29%)
  waiting for transfers between devices  137 us (28%)
  blocking collectives  124 us (25%)
  local copies, waits for them, and re-layouts  32.9 us (7%)
  between operations  23.4 us (5%)
  other arithmetic  19.8 us (4%)
  starting transfers between devices  10.9 us (2%)
    pallas_call x6, Pallas kernels, call(): pl.pallas_call(body, grid=(steps,), in_specs=in_specs, out_specs=tuple((f...  143 us
    reduce_scatter x3, waiting for transfers between devices, scatter(): part = lax.psum_scatter(raw, 'dp', scatter_dimension=0, tiled=False)  84 us
    all_gather x1, blocking collectives, per_device(): everyone = lax.all_gather(packed, ('dp', 'mem'), axis=0, tiled=False)  80.5 us
    all_gather x3, waiting for transfers between devices, gather(): got = lax.all_gather(jnp.stack(parts, 0), 'dp', axis=0, tiled=False)  46.4 us
    psum x1, blocking collectives, per_device(): squares = lax.psum(local, ('dp', 'mem')) + jnp.sum(all_gains * all_gains)  43.1 us
    unnamed x67, local copies, waits for them, and re-layouts  29.1 us
  transfers between devices with their start and end apart: 11, of which 5 were waited for; matrix products, arithmetic and copies ran while one was open for 6% of the time, Pallas kernels for 9%

profile of v1, /device:TPU:12, one launch (start us, length us, event | category | flops | bytes accessed | tf_op | source)
XLA Modules:
  0.0 491.7 jit_solution(5008436786338995991)
XLA Ops:
  7.2 1.7 pad_maximum_fusion
  18.3 5.3 %all-to-all-start = ((bf16[4,256,512]{2,1,0:T(8,128)(2,1)}), bf16[4,256,512]{2,1,0:T(8,128)(2,1)S(1)}, u32[]{:S(2)}, u32[]{:S(2)}) async-start(bf16[4,256,512]{2,1,0:T(8,128)(2,1)} %param.18), calls=%async_computation | async-start | bytes 2097152 | tf_op jit(solution)/shard_map/all_to_all | solution.py:462
  24.4 15.1 %all-gather.9.cloned.1.call-done = bf16[32,64,512]{2,1,0:T(8,128)(2,1)} async-done(((bf16[4,64,512]{2,1,0:T(8,128)(2,1)}), bf16[32,64,512]{2,1,0:T(8,128)(2,1)}) %all-gather.9.cloned.1.call-update) | async-done | bytes 2097168 | tf_op jit(solution)/shard_map/all_gather | solution.py:448
  39.5 1.1 slice.129
  40.7 31.3 %all-gather.11.cloned.1.call-done = bf16[40,64,512]{2,1,0:T(8,128)(2,1)} async-done(((bf16[5,64,512]{2,1,0:T(8,128)(2,1)}), bf16[40,64,512]{2,1,0:T(8,128)(2,1)}) %all-gather.11.cloned.1.call-update) | async-done | bytes 2621456 | tf_op jit(solution)/shard_map/all_gather | solution.py:448
  72.0 21.1 %self_forward.1 = (bf16[1024,512]{1,0:T(8,128)(2,1)S(1)}, bf16[1024,512]{1,0:T(8,128)(2,1)S(1)}, bf16[1024,512]{1,0:T(8,128)(2,1)S(1)}, bf16[1024,512]{1,0:T(8,1...) custom-call(s32[1]{0:T(128)} %constant.12.clone.1.me.me_ref, ...), custom_call_target="tpu_custom_call" | custom-call | flops 14763950080 | bytes 15245316 | tf_op jit(solution)/shard_map/self_forward/pallas_call | solution.py:353
  93.2 1.0 copy-done.14
  94.2 1.0 copy-done.15
  95.1 1.0 copy-done.17
  96.1 1.0 copy-done.19
  97.1 1.0 copy-done.21
  98.1 19.0 %cross_forward.1 = (bf16[1024,512]{1,0:T(8,128)(2,1)S(1)}, bf16[1024,512]{1,0:T(8,128)(2,1)S(1)}, f32[4,2,1024]{2,1,0:T(2,128)S(1)}, bf16[1024,512]{1,0:T(8,128)...) custom-call(s32[1]{0:T(128)} %constant.12.clone.1.me.me_ref, bf16[1024,512]{1,0:T(8,128)(2,1)S(1)} %bitcast.90, ...), custom_call_target="tpu_custom_call" | custom-call | flops 13153337344 | bytes 13146116 | tf_op jit(solution)/shard_map/cross_forward/pallas_call | solution.py:353
  118.1 1.0 copy-done.9
  119.1 1.0 copy-done.11
  120.1 1.6 copy-done.12
  121.7 33.5 %feed_forward.1 = (bf16[1024,512]{1,0:T(8,128)(2,1)}, f32[1024,512]{1,0:T(8,128)S(1)}, bf16[1024,512]{1,0:T(8,128)(2,1)S(1)}, f32[1,512]{1,0:T(1,128)S(1)}, bf16[8,4,512,128]{3,2,1,0:T(8,128)(2,1)}) custom-call(s32[1]{0:T(128)} %constant.12.clone.1.me.me_ref, bf16[1024,512]{1,0:T(8,128)(2,1)S(1)} %copy-done.12, f32[1024,512]{1,0:T(8,128)} %get-tuple-element.47.late, ...), custom_call_target="tpu_custom_call" | custom-call | flops 19327352832 | bytes 16785412 | tf_op jit(solution)/shard_map/feed_forward/pallas_call | solution.py:353
  155.2 1.3 copy-done.13
  156.6 34.9 %cross_back.1 = (bf16[8,4,320,128]{3,2,1,0:T(8,128)(2,1)}, bf16[1024,512]{1,0:T(8,128)(2,1)S(1)}, f32[1024,512]{1,0:T(8,128)}, bf16[1024,512]{1,0:T(8,128)(2,1)S(1)}, f32[1,512]{1,0:T(1,128)S(1)}) custom-call(s32[1]{0:T(128)} %constant.12.clone.1.me.me_ref, bf16[1024,512]{1,0:T(8,128)(2,1)S(1)} %get-tuple-element.49.bt, f32[1024,512]{1,0:T(8,128)} %copy-done.13, ...), custom_call_target="tpu_custom_call" | custom-call | flops 34091302912 | bytes 22061060 | tf_op jit(solution)/shard_map/cross_back/pallas_call | solution.py:353
  191.5 31.4 %self_back.1 = (bf16[8,4,192,128]{3,2,1,0:T(8,128)(2,1)}, f32[1024,512]{1,0:T(8,128)}) custom-call(s32[1]{0:T(128)} %constant.12.clone.1.me.me_ref, bf16[1024,512]{1,0:T(8,128)(2,1)S(1)} %get-tuple-element.58.b1, bf16[1024,512]{1,0:T(8,128)(2,1)S(1)} %copy-done.22, bf16[1024,512]{1,0:T(8,128)(2,1)S(1)} %copy-done.16, bf16[1024,512]{1,0:T(8,128)(2,1)S(1)} %copy-done.18, ...), custom_call_target="tpu_custom_call" | custom-call | flops 32480690176 | bytes 14712836 | tf_op jit(solution)/shard_map/self_back/pallas_call | solution.py:353
  224.1 37.4 %reduce-scatter.7.cloned.1.call-done = bf16[1,4,192,128]{3,2,1,0:T(8,128)(2,1)} async-done(((bf16[8,4,192,128]{3,2,1,0:T(8,128)(2,1)}), bf16[1,4,192,128]{3,2,1,0:T(8,128)(2,1)}) %reduce-scatter.7.cloned.1.call-update) | async-done | bytes 196624 | tf_op jit(solution)/shard_map/reduce_scatter | solution.py:477
  261.8 46.6 %reduce-scatter.11.cloned.1.call-done = bf16[1,4,320,128]{3,2,1,0:T(8,128)(2,1)} async-done(((bf16[8,4,320,128]{3,2,1,0:T(8,128)(2,1)}), bf16[1,4,320,128]{3,2,1,0:T(8,128)(2,1)}) %reduce-scatter.11.cloned.1.call-update) | async-done | bytes 327696 | tf_op jit(solution)/shard_map/reduce_scatter | solution.py:477
  308.4 1.6 copy.35
  310.6 8.3 %reduce.9 = bf16[1024,512]{1,0:T(8,128)(2,1)} reduce(bf16[1024,1,512]{2,1,0:T(2,128)(2,1)S(1)} %bitcast.99, bf16[]{:T(256)} %broadcast.54), dimensions={1}, to_apply=%bitcast.86.reduce_sub_computation | reduce | bytes 2097154
  318.9 4.0 reshape.139
  322.9 5.1 %all-to-all-start.1 = ((bf16[4,2,65536]{2,1,0:T(2,128)(2,1)}), bf16[4,2,65536]{2,1,0:T(2,128)(2,1)}, u32[]{:S(2)}, u32[]{:S(2)}) async-start(bf16[4,2,65536]{2,1,0:T(2,128)(2,1)} %reshape.139), calls=%async_computation.1 | async-start | bytes 2097152 | tf_op jit(solution)/shard_map/all_to_all | solution.py:469
  328.1 1.6 copy-done.1
  329.6 2.6 finish_back.1
  332.3 80.5 %all-gather.4 = f32[32,5,512]{2,1,0:T(8,128)S(1)} all-gather(f32[1,5,512]{2,1,0:T(8,128)S(1)} %maximum_bitcast_fusion), channel_id=5, replica_groups=mesh['dp'=8,'mem'=4] {'dp','mem'}, dimensions={0}, use_global_device_ids=true | all-gather | bytes 337920 | tf_op jit(solution)/shard_map/all_gather | solution.py:493
  414.6 2.6 reshape.140
  426.1 5.7 %reduce-scatter.17.cloned.1.call-done = bf16[1,512,128]{2,1,0:T(8,128)(2,1)} async-done(((bf16[4,512,128]{2,1,0:T(8,128)(2,1)}), bf16[1,512,128]{2,1,0:T(8,128)(2,1)}) %reduce-scatter.17.cloned.1.call-update) | async-done | bytes 131088 | tf_op jit(solution)/shard_map/reduce_scatter | solution.py:478
  435.3 1.3 copy.33
  436.6 43.1 %psum.7 = f32[]{:T(128)} all-reduce(f32[]{:T(128)S(6)} %add.65), channel_id=1, replica_groups=mesh['dp'=8,'mem'=4] {'dp','mem'}, use_global_device_ids=true, to_apply=%region_17.0 | all-reduce | flops 1 | bytes 8 | tf_op jit(solution)/shard_map/psum | solution.py:506
  (108 shorter events, 23.4 us)
Async XLA Ops:
  7.2 10.2 %copy-start.25 = (bf16[256,512]{1,0:T(8,128)(2,1)S(1)}, bf16[256,512]{1,0:T(8,128)(2,1)}, u32[]{:S(2)}) copy-start(bf16[256,512]{1,0:T(8,128)(2,1)} %param.30) | copy-start | bytes 786436
  7.2 32.3 %all-gather.9.cloned.1.call-start = ((), (), s32[]{:S(2)}) async-start(), calls=%async_computation.14 | async-start | bytes 2359296 | tf_op jit(solution)/shard_map/all_gather | solution.py:448
  9.0 63.1 %all-gather.11.cloned.1.call-start = ((), (), s32[]{:S(2)}) async-start(), calls=%async_computation.15 | async-start | bytes 2949120 | tf_op jit(solution)/shard_map/all_gather | solution.py:448
  14.0 106.1 %all-gather.13.cloned.1.call-start = ((), (), s32[]{:S(2)}) async-start(), calls=%async_computation.16 | async-start | bytes 4718592 | tf_op jit(solution)/shard_map/all_gather | solution.py:448
  17.5 54.6 %copy-start.4 = (f32[512,3]{0,1:T(4,128)S(1)}, f32[512,3]{0,1:T(4,128)}, u32[]{:S(2)}) copy-start(f32[512,3]{0,1:T(4,128)} %param.31) | copy-start | bytes 18436
  18.3 79.8 %all-to-all-start = ((bf16[4,256,512]{2,1,0:T(8,128)(2,1)}), bf16[4,256,512]{2,1,0:T(8,128)(2,1)S(1)}, u32[]{:S(2)}, u32[]{:S(2)}) async-start(bf16[4,256,512]{2,1,0:T(8,128)(2,1)} %param.18), calls=%async_computation | async-start | bytes 2097152 | tf_op jit(solution)/shard_map/all_to_all | solution.py:462
  23.6 238.0 %reduce-scatter.7.cloned.1.call-start = ((), (), s32[]{:S(2)}) async-start(), calls=%async_computation.8 | async-start | bytes 1769472 | tf_op jit(solution)/shard_map/reduce_scatter | solution.py:477
  93.2 1.0 copy-start.14
  95.1 1.0 copy-start.17
  96.1 1.0 copy-start.19
  97.1 1.0 copy-start.21
  98.1 19.1 %copy-start.3 = (bf16[4,256,512]{2,1,0:T(8,128)(2,1)}, bf16[4,256,512]{2,1,0:T(8,128)(2,1)S(1)}, u32[]{:S(2)}) copy-start(bf16[4,256,512]{2,1,0:T(8,128)(2,1)S(1)} %all-to-all-done) | copy-start | bytes 3145732
  98.1 22.0 %copy-start.5 = (bf16[1,1024,512]{2,1,0:T(8,128)(2,1)S(1)}, bf16[1,1024,512]{2,1,0:T(8,128)(2,1)}, u32[]{:S(2)}) copy-start(bf16[1,1024,512]{2,1,0:T(8,128)(2,1)} %param.19) | copy-start | bytes 3145732
  118.1 1.0 copy-start.9
  120.1 35.1 %copy-start.7 = (bf16[1024,512]{1,0:T(8,128)(2,1)}, bf16[1024,512]{1,0:T(8,128)(2,1)S(1)}, u32[]{:S(2)}) copy-start(bf16[1024,512]{1,0:T(8,128)(2,1)S(1)} %get-tuple-element.52.k) | copy-start | bytes 3145732
  120.1 1.6 copy-start.12
  121.7 34.8 %copy-start.6 = (bf16[1024,512]{1,0:T(8,128)(2,1)S(1)}, bf16[1024,512]{1,0:T(8,128)(2,1)}, u32[]{:S(2)}) copy-start(bf16[1024,512]{1,0:T(8,128)(2,1)} %get-tuple-element.44.cq) | copy-start | bytes 3145732
  121.7 34.8 %copy-start.10 = (bf16[1024,512]{1,0:T(8,128)(2,1)S(1)}, bf16[1024,512]{1,0:T(8,128)(2,1)}, u32[]{:S(2)}) copy-start(bf16[1024,512]{1,0:T(8,128)(2,1)} %copy-done.9) | copy-start | bytes 3145732
  155.2 1.3 copy-start.13
  156.5 35.0 %copy-start.16 = (bf16[1024,512]{1,0:T(8,128)(2,1)S(1)}, bf16[1024,512]{1,0:T(8,128)(2,1)}, u32[]{:S(2)}) copy-start(bf16[1024,512]{1,0:T(8,128)(2,1)} %copy-done.15) | copy-start | bytes 3145732
  156.5 35.0 %copy-start.18 = (bf16[1024,512]{1,0:T(8,128)(2,1)S(1)}, bf16[1024,512]{1,0:T(8,128)(2,1)}, u32[]{:S(2)}) copy-start(bf16[1024,512]{1,0:T(8,128)(2,1)} %copy-done.17) | copy-start | bytes 3145732
  156.6 35.0 %copy-start.20 = (bf16[1024,512]{1,0:T(8,128)(2,1)S(1)}, bf16[1024,512]{1,0:T(8,128)(2,1)}, u32[]{:S(2)}) copy-start(bf16[1024,512]{1,0:T(8,128)(2,1)} %copy-done.19) | copy-start | bytes 3145732
  156.6 35.0 %copy-start.22 = (bf16[1024,512]{1,0:T(8,128)(2,1)S(1)}, bf16[1024,512]{1,0:T(8,128)(2,1)}, u32[]{:S(2)}) copy-start(bf16[1024,512]{1,0:T(8,128)(2,1)} %copy-done.21) | copy-start | bytes 3145732
  222.9 85.5 %reduce-scatter.11.cloned.1.call-start = ((), (), s32[]{:S(2)}) async-start(), calls=%async_computation.10 | async-start | bytes 2949120 | tf_op jit(solution)/shard_map/reduce_scatter | solution.py:477
  223.5 189.3 %reduce-scatter.15.cloned.1.call-start = ((), (), s32[]{:S(2)}) async-start(), calls=%async_computation.12 | async-start | bytes 4718592 | tf_op jit(solution)/shard_map/reduce_scatter | solution.py:477
  224.1 193.2 %reduce-scatter.9.cloned.1.call-start = ((), (), s32[]{:S(2)}) async-start(), calls=%async_computation.9 | async-start | bytes 245760 | tf_op jit(solution)/shard_map/reduce_scatter | solution.py:478
  261.6 159.7 %reduce-scatter.13.cloned.1.call-start = ((), (), s32[]{:S(2)}) async-start(), calls=%async_computation.11 | async-start | bytes 409600 | tf_op jit(solution)/shard_map/reduce_scatter | solution.py:478
  318.9 9.2 %copy-start = (f32[1024,512]{1,0:T(8,128)S(1)}, f32[1024,512]{1,0:T(8,128)}, u32[]{:S(2)}) copy-start(f32[1024,512]{1,0:T(8,128)} %get-tuple-element.57.refs_2_) | copy-start | bytes 6291460
  318.9 9.2 %copy-start.2 = (bf16[1,1024,512]{2,1,0:T(8,128)(2,1)S(1)}, bf16[1,1024,512]{2,1,0:T(8,128)(2,1)}, u32[]{:S(2)}) copy-start(bf16[1,1024,512]{2,1,0:T(8,128)(2,1)} %param.16) | copy-start | bytes 3145732
  322.9 91.7 %all-to-all-start.1 = ((bf16[4,2,65536]{2,1,0:T(2,128)(2,1)}), bf16[4,2,65536]{2,1,0:T(2,128)(2,1)}, u32[]{:S(2)}, u32[]{:S(2)}) async-start(bf16[4,2,65536]{2,1,0:T(2,128)(2,1)} %reshape.139), calls=%async_computation.1 | async-start | bytes 2097152 | tf_op jit(solution)/shard_map/all_to_all | solution.py:469
  328.0 103.8 %reduce-scatter.17.cloned.1.call-start = ((), (), s32[]{:S(2)}) async-start(), calls=%async_computation.13 | async-start | bytes 655360 | tf_op jit(solution)/shard_map/reduce_scatter | solution.py:478
  328.1 1.6 copy-start.1
  (5 other events, 4.4 us)
Sparse Core Ops, SparseCore 0:
  10.5 28.9 all-gather.8
  41.9 30.0 all-gather.10
  73.9 36.6 all-gather.12
  223.1 38.4 reduce-scatter.6
  264.7 43.6 reduce-scatter.10
  311.6 51.4 reduce-scatter.14
  365.5 17.0 reduce-scatter.8
  384.9 18.8 reduce-scatter.12
  413.0 18.8 reduce-scatter.16
